TPU v7x, 256 devices: a whole 4x4x8 slice. The times are simulated.
256 devices in a mesh: attn: 16 (over y, x), expert: 8 (over z), tp: 2 (over core).
Axes of the slice: x: 4, y: 4, z: 8, core: 2. Of those that a mesh axis runs over, the one named last changes fastest.
Arguments:
- tokens: bfloat16 [32, 6144], P('expert', 'attn'), may hold values from -6 to 6
- queries: bfloat16 [32, 48, 128], P(('attn', 'tp'), 'expert'), may hold values from -120 to 120
- key_cache: bfloat16 [32, 8, 4096, 128], P(('attn', 'tp'), 'expert'), may hold values from -6 to 6
- value_cache: bfloat16 [32, 8, 4096, 128], P(('attn', 'tp'), 'expert'), may hold values from -6 to 6
- lengths: int32 [32], P(('attn', 'tp')), may hold values from 2 to 4096, as said below
- out_weight: bfloat16 [6144, 6144], P('expert', 'attn'), may hold values from -1.75 to 1.75
- norm_gain: bfloat16 [6144], P('attn'), may hold values from 0.099609375 to 1.8984375
- router_weight: float32 [6144, 8], P('attn'), may hold values from -0.15625 to 0.15625
- routes: int32 [32, 2], P('expert'), may hold values from 0 to 7, all different within a row; in each aligned block of 4 rows (0 to 3, 4 to 7, ...) at most 3 rows name the same one
- up_weight: bfloat16 [8, 6144, 2, 8192], P('expert', None, None, ('attn', 'tp')), may hold values from -0.078125 to 0.078125
- down_weight: bfloat16 [8, 8192, 6144], P('expert', ('attn', 'tp')), may hold values from -0.0625 to 0.0625
Outputs:
- mixed: bfloat16 [32, 6144], P('expert', 'attn')
Inputs may be any that keep to these rules, and one draw needn't show every extreme that they name: Row r's live slots are 0 to lengths[r] - 1; some row has all 4096 slots live. `routes`: the two experts of a row differ; within the rows of one index of expert no expert is named by more than 3 rows, a bound that some block reaches.
All inputs are finite; a program needn't handle non-finite values.
Results may differ from a plain program's by a relative error of at most 0.02.
Values may be sent and summed in bfloat16 or wider, within the bound.
A program may use at most 64 MiB of HBM per device.

v0:
```python
import jax
import jax.numpy as jnp
from jax import lax
from jax.sharding import PartitionSpec as P

D = 6144
ROW_DEV = 1


def attend_row(query, keys, values, length):
    group = query.shape[0] // keys.shape[0]
    grouped = query.reshape(keys.shape[0], group, keys.shape[2])
    scores = jnp.einsum(
        "kgd,ktd->kgt", grouped, keys, preferred_element_type=jnp.float32
    ) * keys.shape[2] ** (-0.5)
    live = jnp.arange(keys.shape[1]) < length
    scores = jnp.where(live[None, None, :], scores, -jnp.inf)
    top = jnp.max(scores, axis=2, keepdims=True)
    weights = jnp.exp(scores - top)
    total = jnp.sum(weights, axis=2, keepdims=True)
    probs = (weights / total).astype(jnp.bfloat16)
    mixed = jnp.einsum("kgt,ktd->kgd", probs, values, preferred_element_type=jnp.float32)
    return mixed.reshape(-1).astype(jnp.bfloat16)


def shards(
    tokens,
    queries,
    key_cache,
    value_cache,
    lengths,
    out_weight,
    norm_gain,
    router_weight,
    routes,
    up_weight,
    down_weight,
):
    heads = jax.vmap(attend_row)(queries, key_cache, value_cache, lengths)
    gathered = lax.all_gather(heads, ("attn", "tp"), axis=0, tiled=True)
    block = tokens.shape[0]
    attended = lax.psum_scatter(
        jnp.dot(gathered, out_weight, preferred_element_type=jnp.float32).astype(jnp.bfloat16),
        "expert",
        scatter_dimension=0,
        tiled=True,
    ).astype(jnp.float32)
    resid = lax.optimization_barrier((tokens.astype(jnp.float32) + attended).astype(jnp.bfloat16))
    wide = resid.astype(jnp.float32)
    gained = wide * norm_gain.astype(jnp.float32)
    squares = jnp.sum(wide * wide, axis=1)
    partial_logits = jnp.dot(gained, router_weight, precision=lax.Precision.HIGHEST)
    squares, logits = lax.psum((squares, partial_logits), "attn")
    scale = lax.rsqrt(squares / D + 1e-05)[:, None]
    normed = (gained * scale).astype(jnp.bfloat16)
    logits = logits * scale
    chosen = jnp.take_along_axis(logits, routes, axis=1)
    gates = jax.nn.sigmoid(
        jnp.stack([chosen[:, 0] - chosen[:, 1], chosen[:, 1] - chosen[:, 0]], axis=1)
    )
    experts = router_weight.shape[1]
    n_groups = lax.axis_size("expert")
    local = experts // n_groups
    cap = min(3 * ROW_DEV, block)
    flat = routes.reshape(-1)
    marks = (flat[:, None] == jnp.arange(experts)[None, :]).astype(jnp.int32)
    before = jnp.cumsum(marks, axis=0) - marks
    place = jnp.sum(before * marks, axis=1)
    slot = flat * cap + place
    table = (slot[None, :] == jnp.arange(experts * cap)[:, None]).astype(jnp.float32)
    table = table.reshape(experts * cap, block, routes.shape[1])
    pick = jnp.sum(table, axis=2).astype(jnp.bfloat16)
    combine = jnp.einsum("sbk,bk->bs", table, gates, precision=lax.Precision.HIGHEST)
    packed = jnp.dot(pick, normed, preferred_element_type=jnp.float32).astype(jnp.bfloat16)
    arrived = lax.all_to_all(
        packed.reshape(n_groups, local * cap, -1), "expert", split_axis=0, concat_axis=0, tiled=True
    )
    arrived = lax.all_gather(arrived, "attn", axis=2, tiled=True)
    inputs = (
        arrived.reshape(n_groups, local, cap, -1)
        .transpose(1, 0, 2, 3)
        .reshape(local, n_groups * cap, -1)
    )
    both = jnp.einsum("esd,edcf->escf", inputs, up_weight, preferred_element_type=jnp.float32)
    hidden = (jax.nn.silu(both[:, :, 0]) * both[:, :, 1]).astype(jnp.bfloat16)
    partial_value = jnp.einsum(
        "esf,efd->esd", hidden, down_weight, preferred_element_type=jnp.float32
    )
    share = lax.psum(partial_value.astype(jnp.bfloat16), "tp").astype(jnp.float32)
    share = lax.psum_scatter(
        share.astype(jnp.bfloat16), "attn", scatter_dimension=2, tiled=True
    ).astype(jnp.float32)
    outputs = share.astype(jnp.bfloat16).reshape(local, n_groups, cap, -1)
    outputs = outputs.transpose(1, 0, 2, 3).reshape(n_groups, local * cap, -1)
    returned = lax.all_to_all(outputs, "expert", split_axis=0, concat_axis=0, tiled=True)
    flat_back = returned.reshape(experts * cap, -1).astype(jnp.float32)
    moe = jnp.dot(combine, flat_back, precision=lax.Precision.HIGHEST)
    return (wide + moe).astype(jnp.bfloat16)


def solution(mesh):
    placed = (
        P("expert", "attn"),
        P(("attn", "tp"), "expert", None),
        P(("attn", "tp"), "expert", None, None),
        P(("attn", "tp"), "expert", None, None),
        P(("attn", "tp")),
        P("expert", "attn"),
        P("attn"),
        P("attn", None),
        P("expert", None),
        P("expert", None, None, ("attn", "tp")),
        P("expert", ("attn", "tp"), None),
    )
    return jax.shard_map(
        shards, mesh=mesh, in_specs=placed, out_specs=P("expert", "attn"), check_vma=False
    )
```

profile of v0, /device:TPU:1, one launch (start us, length us, event | category | flops | bytes accessed | tf_op | source)
XLA Modules:
  0.0 260.0 jit_solution(2947147637039599581)
XLA Ops:
  7.3 0.9 copy.37
  8.3 0.7 convert_element_type.84
  9.1 0.2 select_reduce_fusion
  9.6 1.7 fusion.36
  11.3 0.2 fusion.11
  11.6 1.5 convolution_convert_fusion.3
  13.1 26.1 %all-gather = bf16[32,1,768]{2,1,0:T(2,128)(2,1)S(1)} all-gather(bf16[1,1,768]{2,1,0:T(2,128)(2,1)S(1)} %reshape.152), channel_id=1, replica_groups=mesh['attn'=16,'expert'=8,'tp'=2] {'attn','tp'}, dimensions={0}, use_global_device_ids=true | all-gather | bytes 50688 | tf_op jit(solution)/shard_map/all_gather | solution.py:40
  39.2 1.3 convolution_convert_fusion.1
  40.5 25.8 %all-reduce = bf16[32,384]{1,0:T(8,128)(2,1)S(1)} all-reduce(bf16[32,384]{1,0:T(8,128)(2,1)S(1)} %convolution_convert_fusion.1), channel_id=2, replica_groups=mesh['attn'=16,'expert'=8,'tp'=2] {'expert'}, use_global_device_ids=true, to_apply=%region_2.3.clone | all-reduce | flops 12288 | bytes 49152
  66.3 0.6 dynamic-slice
  67.5 0.1 fusion.24
  67.7 0.1 fusion.22
  67.8 30.8 %all-reduce.1 = (f32[4,8]{1,0:T(4,128)S(1)}, f32[4]{0:T(128)S(1)}) all-reduce(f32[4,8]{1,0:T(4,128)S(1)} %fusion.22, f32[4]{0:T(128)S(1)} %fusion.24), channel_id=1, replica_groups=mesh['attn'=16,'expert'=8,'tp'=2] {'attn'}, use_global_device_ids=true, to_apply=%region_5.6 | all-reduce | flops 36 | bytes 288 | tf_op jit(solution)/shard_map/psum | solution.py:53
  98.6 0.2 convolution_convert_fusion.2
  98.8 0.6 reshape.136
  99.4 3.9 %all-to-all-start = ((bf16[8,3,384]{2,1,0:T(4,128)(2,1)}), bf16[8,3,384]{2,1,0:T(4,128)(2,1)}, u32[]{:S(2)}, u32[]{:S(2)}) async-start(bf16[8,3,384]{2,1,0:T(4,128)(2,1)} %reshape.136), calls=%async_computation | async-start | bytes 49152 | tf_op jit(solution)/shard_map/all_to_all | solution.py:75
  103.7 0.7 gather_fusion
  104.5 5.6 %all-to-all-done = bf16[8,3,384]{2,1,0:T(4,128)(2,1)} async-done(((bf16[8,3,384]{2,1,0:T(4,128)(2,1)}), bf16[8,3,384]{2,1,0:T(4,128)(2,1)}, u32[]{:S(2)}, u32[]{:S(2)}) %all-to-all-start) | async-done | bytes 18464 | tf_op jit(solution)/shard_map/all_to_all | solution.py:75
  110.1 16.7 %all_gather.7 = bf16[8,3,6144]{2,1,0:T(4,128)(2,1)S(1)} all-gather(bf16[8,3,384]{2,1,0:T(4,128)(2,1)} %all-to-all-done), channel_id=1, replica_groups=mesh['attn'=16,'expert'=8,'tp'=2] {'attn'}, dimensions={2}, use_global_device_ids=true | all-gather | bytes 313344 | tf_op jit(solution)/shard_map/all_gather | solution.py:78
  126.8 1.0 reshape.157
  127.8 3.8 %fusion.5 = f32[1,24,2,256]{3,1,2,0:T(8,128)S(1)} fusion(bf16[24,6144,1]{1,0,2:T(8,128)(2,1)} %reshape.157, bf16[6144,2,256]{2,1,0:T(2,128)(2,1)} %bitcast.56), kind=kOutput, calls=%fused_computation.9 | convolution fusion | flops 150994944 | bytes 6635520 | tf_op jit(solution)/shard_map/esd,edcf->escf/dot_general | solution.py:84
  131.6 0.5 fusion
  132.1 5.0 %copy.49 = bf16[1,24,6144]{1,0,2:T(2,128)(2,1)} copy(bf16[1,24,6144]{2,1,0:T(8,128)(2,1)S(1)} %fusion) | data formatting | bytes 589824
  137.2 3.2 %copy.64 = bf16[6144,1,24]{2,0,1:T(8,128)(2,1)} copy(bf16[6144,1,24]{2,1,0:T(2,128)(2,1)} %bitcast.52) | data formatting | bytes 589824
  140.7 91.1 %reduce-scatter.4.cloned.1.call-done = bf16[384,24]{1,0:T(8,128)(2,1)} async-done(((bf16[6144,24]{1,0:T(8,128)(2,1)}), bf16[384,24]{1,0:T(8,128)(2,1)}) %reduce-scatter.4.cloned.1.call-update) | async-done | bytes 18448
  231.8 1.0 reshape_bitcast_fusion
  232.9 5.5 %psum.24 = bf16[1,24,384]{2,1,0:T(8,128)(2,1)S(1)} all-reduce(bf16[1,24,384]{2,1,0:T(8,128)(2,1)S(1)} %copy.50), channel_id=1, replica_groups=mesh['attn'=16,'expert'=8,'tp'=2] {'tp'}, use_global_device_ids=true, to_apply=%region_9.10 | all-reduce | flops 9216 | bytes 36864 | tf_op jit(solution)/shard_map/psum | solution.py:89
  238.4 0.6 reshape_transpose_reshape.4
  239.0 6.7 %all-to-all-start.1 = ((bf16[8,3,384]{2,1,0:T(4,128)(2,1)}), bf16[8,3,384]{2,1,0:T(4,128)(2,1)S(1)}, u32[]{:S(2)}, u32[]{:S(2)}) async-start(bf16[8,3,384]{2,1,0:T(4,128)(2,1)} %reshape_transpose_reshape.4), calls=%async_computation.1 | async-start | bytes 49152 | tf_op jit(solution)/shard_map/all_to_all | solution.py:95
  245.7 0.1 fusion.19
  245.9 6.5 %all-to-all-done.1 = bf16[8,3,384]{2,1,0:T(4,128)(2,1)S(1)} async-done(((bf16[8,3,384]{2,1,0:T(4,128)(2,1)}), bf16[8,3,384]{2,1,0:T(4,128)(2,1)S(1)}, u32[]{:S(2)}, u32[]{:S(2)}) %all-to-all-start.1) | async-done | bytes 18464 | tf_op jit(solution)/shard_map/all_to_all | solution.py:95
  252.4 0.7 fusion.8
  (33 shorter events, 1.4 us)
Async XLA Ops:
  6.5 125.1 %copy-start = (bf16[1,256,6144]{2,1,0:T(8,128)(2,1)S(1)}, bf16[1,256,6144]{2,1,0:T(8,128)(2,1)}, u32[]{:S(2)}) copy-start(bf16[1,256,6144]{2,1,0:T(8,128)(2,1)} %param.21) | copy-start | bytes 9437188
  6.5 59.7 %copy-start.3 = (u32[256]{0:T(256)S(1)}, u32[256]{0:T(256)}, u32[]{:S(2)}) copy-start(u32[256]{0:T(256)} %constant.61) | copy-start | bytes 3076
  6.5 61.0 %copy-start.2 = (bf16[4,384]{1,0:T(4,128)(2,1)S(1)}, bf16[4,384]{1,0:T(4,128)(2,1)}, u32[]{:S(2)}) copy-start(bf16[4,384]{1,0:T(4,128)(2,1)} %param.11) | copy-start | bytes 9220
  6.5 61.1 %copy-start.1 = (f32[384,8]{0,1:T(8,128)S(1)}, f32[384,8]{0,1:T(8,128)}, u32[]{:S(2)}) copy-start(f32[384,8]{0,1:T(8,128)} %param.18) | copy-start | bytes 36868
  99.4 10.7 %all-to-all-start = ((bf16[8,3,384]{2,1,0:T(4,128)(2,1)}), bf16[8,3,384]{2,1,0:T(4,128)(2,1)}, u32[]{:S(2)}, u32[]{:S(2)}) async-start(bf16[8,3,384]{2,1,0:T(4,128)(2,1)} %reshape.136), calls=%async_computation | async-start | bytes 49152 | tf_op jit(solution)/shard_map/all_to_all | solution.py:75
  103.3 128.4 %reduce-scatter.4.cloned.1.call-start = ((), (), s32[]{:S(2)}) async-start(), calls=%async_computation.3 | async-start | bytes 1671168
  239.0 13.4 %all-to-all-start.1 = ((bf16[8,3,384]{2,1,0:T(4,128)(2,1)}), bf16[8,3,384]{2,1,0:T(4,128)(2,1)S(1)}, u32[]{:S(2)}, u32[]{:S(2)}) async-start(bf16[8,3,384]{2,1,0:T(4,128)(2,1)} %reshape_transpose_reshape.4), calls=%async_computation.1 | async-start | bytes 49152 | tf_op jit(solution)/shard_map/all_to_all | solution.py:95
Sparse Core Ops, SparseCore 0:
  140.6 91.1 reduce-scatter.3
where the time goes:
time: 261 us; the launch traced here: 260 us
  blocking collectives  105 us (40%)
  waiting for transfers between devices  103 us (39%)
  between operations  14.9 us (6%)
  local copies, waits for them, and re-layouts  14.4 us (6%)
  starting transfers between devices  10.7 us (4%)
  matrix products  10 us (4%)
    unnamed x2, waiting for transfers between devices  91.1 us
    psum x1, blocking collectives, shards(): squares, logits = lax.psum((squares, partial_logits), 'attn')  30.8 us
    all_gather x1, blocking collectives, shards(): gathered = lax.all_gather(heads, ('attn', 'tp'), axis=0, tiled=True)  26.1 us
    unnamed x1, blocking collectives  25.8 us
    all_gather x1, blocking collectives, shards(): arrived = lax.all_gather(arrived, 'attn', axis=2, tiled=True)  16.7 us
    unnamed x15, local copies, waits for them, and re-layouts  10.9 us
    all_to_all x1, starting transfers between devices, shards(): lax.all_to_all(outputs, 'expert', split_axis=0, concat_axis=0, tiled=True)  6.74 us
    all_to_all x1, waiting for transfers between devices, shards(): lax.all_to_all(outputs, 'expert', split_axis=0, concat_axis=0, tiled=True)  6.54 us
  transfers between devices with their start and end apart: 3, of which 3 were waited for; matrix products, arithmetic and copies ran while one was open for 1% of the time, Pallas kernels for 0%

commit v1 on v0

v1 whole, which is shorter than its diff:
```python
import jax
import jax.numpy as jnp
from jax import lax
from jax.experimental import pallas as pl
from jax.experimental.pallas import tpu as pltpu
from jax.sharding import PartitionSpec as P

MESH = pl.DeviceIdType.MESH
F32, BF16 = jnp.float32, jnp.bfloat16
D = 6144
HD = 128
GROUP = 6
CACHE = 4096
NA, NE, NT = 16, 8, 2
HALF = 16
COLS = 384
HID = 256
NEAR = sorted(
    ((dy, dx) for dy in range(4) for dx in range(4)),
    key=lambda o: min(o[0], 4 - o[0]) + min(o[1], 4 - o[1]),
)


def drain(ref, sem):
    pltpu.make_async_copy(ref, ref, sem).wait()


def kernel(
    tok_hbm, q_hbm, k_hbm, v_hbm, len_ref, wo_hbm, gain_hbm, router_hbm, routes_hbm, up_hbm, down_hbm,
    out_ref,
    tok, q, k, v, wo, gain, router, routes, up, up2, down,
    heads, gath, zsum, resid, feats, stat, stats, stat_tot, hid, part, part_sib, reduced, back, ret_s, ret,
    in_sem, p1_s, p1_r, p2_s, p2_r, p3_s, p3_r, fw_s, fw_r, st_s, st_r, sib_s, sib_r, p4x_s, p4x_r, p4_s, p4_r, p5_s, p5_r,
):
    a, e, t = lax.axis_index("attn"), lax.axis_index("expert"), lax.axis_index("tp")
    ay, ax = lax.div(a, 4), lax.rem(a, 4)
    sib = (a, e, 1 - t)

    def near(o):
        return lax.rem(ay + o[0], 4) * 4 + lax.rem(ax + o[1], 4)

    loads = {}
    pairs = (
        ("q", q_hbm, q), ("k", k_hbm, k), ("v", v_hbm, v), ("wo", wo_hbm, wo), ("tok", tok_hbm, tok),
        ("gain", gain_hbm, gain), ("router", router_hbm, router), ("routes", routes_hbm, routes),
        ("up", up_hbm, up), ("down", down_hbm, down),
    )
    for n, (name, src, dst) in enumerate(pairs):
        loads[name] = pltpu.make_async_copy(src, dst, in_sem.at[n])
        loads[name].start()

    barrier = pltpu.get_barrier_semaphore()

    def greet_plane(j, c):
        other = lax.rem(2 * a + t + 1 + j, 32)
        pl.semaphore_signal(
            barrier, inc=1, device_id=(lax.div(other, 2), e, lax.rem(other, 2)), device_id_type=MESH
        )
        return c

    def greet_z(j, c):
        other = lax.rem(2 * e + t + 2 + j, 16)
        pl.semaphore_signal(
            barrier, inc=1, device_id=(a, lax.rem(e + 1 + lax.div(j, 2), NE), lax.rem(other, 2)), device_id_type=MESH
        )
        return c

    lax.fori_loop(0, 31, greet_plane, 0)
    lax.fori_loop(0, 14, greet_z, 0)

    loads["q"].wait()
    loads["k"].wait()
    scores = lax.dot_general(
        q[...], k[...], (((1,), (1,)), ((), ())), preferred_element_type=F32
    ) * (HD**-0.5)
    live = lax.broadcasted_iota(jnp.int32, scores.shape, 1) < len_ref[0]
    scores = jnp.where(live, scores, -jnp.inf)
    weights = jnp.exp(scores - jnp.max(scores, axis=1, keepdims=True))
    total = jnp.sum(weights, axis=1, keepdims=True)
    probs = (weights / total).astype(BF16)
    loads["v"].wait()
    mixed = jnp.dot(probs, v[...], preferred_element_type=F32)
    heads[...] = jnp.zeros_like(heads)
    heads[0:GROUP, :] = mixed

    pl.semaphore_wait(barrier, 45)

    half = lax.div(a, 8)
    slot = 2 * lax.rem(a, 8) + t

    def send_heads(o):
        pltpu.make_async_remote_copy(
            src_ref=heads, dst_ref=gath.at[slot], send_sem=p1_s, recv_sem=p1_r,
            device_id=(near(o), e, half), device_id_type=MESH,
        ).start()

    for o in NEAR[:0:-1]:
        send_heads(o)

    @pl.when(half != t)
    def _():
        send_heads((0, 0))

    @pl.when(half == t)
    def _():
        gath[slot] = heads[...]

    loads["up"].wait()

    def relayout(i, c):
        s = pl.ds(pl.multiple_of(i * COLS, COLS), COLS)
        up2[:, s, :] = jnp.swapaxes(up[s].astype(F32), 0, 1).astype(BF16)
        return c

    lax.fori_loop(0, D // COLS, relayout, 0)
    for name in ("wo", "tok", "gain", "router", "routes", "down"):
        loads[name].wait()
    mine = lax.broadcasted_iota(jnp.int32, (HALF, COLS), 0) // 4 == e - 4 * t
    tokens = jnp.where(mine, jnp.concatenate([tok[...].astype(F32)] * 4, axis=0), 0.0)

    @pl.when(half == t)
    def _():
        drain(gath.at[pl.ds(0, 15)], p1_r)

    @pl.when(half != t)
    def _():
        drain(gath, p1_r)

    flat = jnp.concatenate([gath[:, h, :].astype(BF16) for h in range(GROUP)], axis=1)
    projected = jnp.dot(flat, wo[...], preferred_element_type=F32) + tokens
    zsum[e] = projected.astype(BF16)

    for dz in (4, 3, 5, 2, 6, 1, 7):
        pltpu.make_async_remote_copy(
            src_ref=zsum.at[e], dst_ref=zsum.at[e], send_sem=p2_s, recv_sem=p2_r,
            device_id=(a, lax.rem(e + dz, NE), t), device_id_type=MESH,
        ).start()
    gains = gain[...].reshape(1, COLS).astype(F32)
    drain(zsum.at[pl.ds(0, 7)], p2_r)
    rounded = sum(zsum[i].astype(F32) for i in range(NE)).astype(BF16)
    wide = rounded.astype(F32)
    gained = wide * gains
    feats[a, t] = gained.astype(BF16)

    def feature_copy(o):
        return pltpu.make_async_remote_copy(
            src_ref=feats.at[a, t], dst_ref=feats.at[a, t], send_sem=p3_s, recv_sem=p3_r.at[a],
            device_id=(near(o), e, t), device_id_type=MESH,
        )

    def forward_copy(o):
        b = near(o)
        return pltpu.make_async_remote_copy(
            src_ref=feats.at[b, t], dst_ref=feats.at[b, t], send_sem=fw_s, recv_sem=fw_r.at[b],
            device_id=sib, device_id_type=MESH,
        )

    for o in NEAR[:0:-1]:
        feature_copy(o).start()
    forward_copy((0, 0)).start()
    resid[t] = rounded
    resid_copy = pltpu.make_async_remote_copy(
        src_ref=resid.at[t], dst_ref=resid.at[t], send_sem=sib_s.at[0], recv_sem=sib_r.at[0],
        device_id=sib, device_id_type=MESH,
    )
    resid_copy.start()

    lane = lax.broadcasted_iota(jnp.int32, (HALF, 128), 1)
    table = jnp.where(lane == 8, jnp.sum(wide * wide, axis=1, keepdims=True), 0.0)
    for x in range(NE):
        table = table + jnp.where(
            lane == x, jnp.sum(gained * router[x : x + 1, :], axis=1, keepdims=True), 0.0
        )
    stat[...] = table[0:8] + pltpu.roll(table[8:16], 64, 1)
    for o in NEAR[:0:-1]:
        pltpu.make_async_remote_copy(
            src_ref=stat, dst_ref=stats.at[a], send_sem=st_s, recv_sem=st_r,
            device_id=(near(o), e, t), device_id_type=MESH,
        ).start()
    stats[a] = stat[...]

    gate_acc = jnp.zeros((2 * HALF, HID), F32)
    up_acc = jnp.zeros((2 * HALF, HID), F32)

    def chunk(o, gate_acc, up_acc):
        b = near(o)
        drain(feats.at[b, 1 - t], fw_r.at[b])
        x = jnp.concatenate([feats[b, 0], feats[b, 1]], axis=0)
        s = pl.ds(pl.multiple_of(b * COLS, COLS), COLS)
        gate_acc = gate_acc + jnp.dot(x, up2[0, s, :], preferred_element_type=F32)
        up_acc = up_acc + jnp.dot(x, up2[1, s, :], preferred_element_type=F32)
        return gate_acc, up_acc

    LAG = 2
    for j, o in enumerate(NEAR):
        if j > 0:
            drain(feats.at[near(o), t], p3_r.at[near(o)])
            forward_copy(o).start()
        if j >= LAG:
            gate_acc, up_acc = chunk(NEAR[j - LAG], gate_acc, up_acc)
    drain(stats.at[pl.ds(0, 15)], st_r)
    stat_tot[t] = sum(stats[i] for i in range(NA))
    total_copy = pltpu.make_async_remote_copy(
        src_ref=stat_tot.at[t], dst_ref=stat_tot.at[t], send_sem=sib_s.at[1], recv_sem=sib_r.at[1],
        device_id=sib, device_id_type=MESH,
    )
    total_copy.start()
    for o in NEAR[NA - LAG :]:
        gate_acc, up_acc = chunk(o, gate_acc, up_acc)
    drain(stat_tot.at[1 - t], sib_r.at[1])
    tots = jnp.concatenate(
        [stat_tot[0], pltpu.roll(stat_tot[0], 64, 1), stat_tot[1], pltpu.roll(stat_tot[1], 64, 1)], axis=0
    )
    scale = lax.rsqrt(tots[:, 8:9] / D + 1e-05)
    gate_acc, up_acc = gate_acc * scale, up_acc * scale
    hidden = (gate_acc * jax.nn.sigmoid(gate_acc) * up_acc).astype(BF16)
    hid[...] = hidden

    def pair_copy(c):
        s = pl.ds(4 * c, 4)
        return pltpu.make_async_remote_copy(
            src_ref=part.at[1 - t, s], dst_ref=part_sib.at[s], send_sem=p4x_s, recv_sem=p4x_r.at[c],
            device_id=sib, device_id_type=MESH,
        )

    order = [lax.rem(ay + g, 4) for g in (2, 1, 3, 0)]
    for c in order:
        s = pl.ds(pl.multiple_of(c * (4 * COLS), 4 * COLS), 4 * COLS)
        d = jnp.dot(hid[...], down[:, s], preferred_element_type=F32).astype(BF16)
        for i in range(4):
            part[0, 4 * c + i] = d[0:HALF, i * COLS : (i + 1) * COLS]
            part[1, 4 * c + i] = d[HALF:, i * COLS : (i + 1) * COLS]
        pair_copy(c).start()
    for c in order:
        drain(part_sib.at[pl.ds(4 * c, 4)], p4x_r.at[c])
        for g in (2, 1, 3, 0):
            b = 4 * c + lax.rem(ax + g, 4)
            reduced[b] = (part[t, b].astype(F32) + part_sib[b].astype(F32)).astype(BF16)

            @pl.when(b != a)
            def _():
                pltpu.make_async_remote_copy(
                    src_ref=reduced.at[b], dst_ref=back.at[a], send_sem=p4_s, recv_sem=p4_r,
                    device_id=(b, e, t), device_id_type=MESH,
                ).start()

    back[a] = reduced[a]

    logits = tots * scale
    own = sum(jnp.where(e == i, logits[4 * i : 4 * i + 4], 0.0) for i in range(NE))
    square = (4, 128)
    lanes = lax.broadcasted_iota(jnp.int32, square, 1)
    rows = lax.broadcasted_iota(jnp.int32, (4, 4), 0)
    diag = lax.broadcasted_iota(jnp.int32, (4, 4), 1) == rows
    names = [
        jnp.sum(jnp.where(diag, jnp.broadcast_to(routes[n : n + 1, :], (4, 4)), 0), axis=1, keepdims=True)
        for n in range(2)
    ]
    chosen = [jnp.sum(jnp.where(lanes == names[n], own, 0.0), axis=1, keepdims=True) for n in range(2)]
    gates = [jax.nn.sigmoid(chosen[0] - chosen[1]), jax.nn.sigmoid(chosen[1] - chosen[0])]
    drain(resid.at[1 - t], sib_r.at[0])
    base = jnp.zeros((4, COLS), F32)
    for h in range(2):
        both = resid[h].astype(F32)
        for i in range(4):
            base = base + jnp.where(e == 4 * h + i, both[4 * i : 4 * i + 4], 0.0)

    drain(back.at[pl.ds(0, 15)], p4_r)
    summed = sum(back[i].astype(F32) for i in range(NA))

    for i in range(4):
        ret_s[i] = summed[4 * i : 4 * i + 4]
    for i in range(4):
        for other in range(2):
            row_owner = 4 * t + i
            itself = jnp.logical_and(row_owner == e, other == t)

            @pl.when(jnp.logical_not(itself))
            def _():
                pltpu.make_async_remote_copy(
                    src_ref=ret_s.at[i], dst_ref=ret.at[e], send_sem=p5_s, recv_sem=p5_r,
                    device_id=(a, row_owner, other), device_id_type=MESH,
                ).start()

            @pl.when(itself)
            def _():
                ret[e] = ret_s[i]

    home = lax.div(e, 4) == t

    @pl.when(home)
    def _():
        drain(ret.at[pl.ds(0, 7)], p5_r)
        drain(ret.at[pl.ds(0, 7)], p5_s)

    @pl.when(jnp.logical_not(home))
    def _():
        drain(ret, p5_r)
        drain(ret, p5_s)

    for x in range(NE):
        share = sum(jnp.where(names[n] == x, gates[n], 0.0) for n in range(2))
        base = base + share * ret[x]
    out_ref[...] = base.astype(BF16)

    @pl.when(half == t)
    def _():
        drain(gath.at[pl.ds(0, 15)], p1_s)

    @pl.when(half != t)
    def _():
        drain(gath, p1_s)

    drain(zsum.at[pl.ds(0, 7)], p2_s)
    drain(back.at[pl.ds(0, 15)], p3_s)
    drain(back, fw_s)
    drain(stats.at[pl.ds(0, 15)], st_s)
    drain(resid.at[t], sib_s.at[0])
    drain(stat_tot.at[t], sib_s.at[1])
    drain(part_sib, p4x_s)
    drain(back.at[pl.ds(0, 15)], p4_s)


def shards(
    tokens, queries, key_cache, value_cache, lengths, out_weight, norm_gain, router_weight, routes, up_weight, down_weight
):
    hbm = pl.BlockSpec(memory_space=pl.ANY)
    dma = pltpu.SemaphoreType.DMA
    return pl.pallas_call(
        kernel,
        out_shape=jax.ShapeDtypeStruct((4, COLS), BF16),
        in_specs=[hbm] * 4 + [pl.BlockSpec(memory_space=pltpu.SMEM)] + [hbm] * 6,
        out_specs=pl.BlockSpec(memory_space=pltpu.VMEM),
        scratch_shapes=[
            pltpu.VMEM((4, COLS), BF16),
            pltpu.VMEM((GROUP, HD), BF16),
            pltpu.VMEM((CACHE, HD), BF16),
            pltpu.VMEM((CACHE, HD), BF16),
            pltpu.VMEM((GROUP * HD, COLS), BF16),
            pltpu.VMEM((COLS,), BF16),
            pltpu.VMEM((NE, COLS), F32),
            pltpu.VMEM((2, 4), jnp.int32),
            pltpu.VMEM((D, 2, HID), BF16),
            pltpu.VMEM((2, D, HID), BF16),
            pltpu.VMEM((HID, D), BF16),
            pltpu.VMEM((8, HD), F32),
            pltpu.VMEM((HALF, 8, HD), F32),
            pltpu.VMEM((NE, HALF, COLS), BF16),
            pltpu.VMEM((NT, HALF, COLS), BF16),
            pltpu.VMEM((NA, NT, HALF, COLS), BF16),
            pltpu.VMEM((8, 128), F32),
            pltpu.VMEM((NA, 8, 128), F32),
            pltpu.VMEM((NT, 8, 128), F32),
            pltpu.VMEM((2 * HALF, HID), BF16),
            pltpu.VMEM((NT, NA, HALF, COLS), BF16),
            pltpu.VMEM((NA, HALF, COLS), BF16),
            pltpu.VMEM((NA, HALF, COLS), BF16),
            pltpu.VMEM((NA, HALF, COLS), BF16),
            pltpu.VMEM((4, 4, COLS), F32),
            pltpu.VMEM((NE, 4, COLS), F32),
            dma((10,)),
            dma, dma, dma, dma, dma, dma((NA,)), dma, dma((NA,)), dma, dma,
            dma((2,)), dma((2,)), dma, dma((4,)), dma, dma, dma, dma,
        ],
        compiler_params=pltpu.CompilerParams(
            collective_id=0, has_side_effects=True, vmem_limit_bytes=63 << 20
        ),
    )(
        tokens,
        queries.reshape(GROUP, HD),
        key_cache.reshape(CACHE, HD),
        value_cache.reshape(CACHE, HD),
        lengths,
        out_weight,
        norm_gain,
        router_weight.T,
        routes.T,
        up_weight.reshape(D, 2, HID),
        down_weight.reshape(HID, D),
    )


def solution(mesh):
    placed = (
        P("expert", "attn"),
        P(("attn", "tp"), "expert", None),
        P(("attn", "tp"), "expert", None, None),
        P(("attn", "tp"), "expert", None, None),
        P(("attn", "tp")),
        P("expert", "attn"),
        P("attn"),
        P("attn", None),
        P("expert", None),
        P("expert", None, None, ("attn", "tp")),
        P("expert", ("attn", "tp"), None),
    )
    return jax.shard_map(
        shards, mesh=mesh, in_specs=placed, out_specs=P("expert", "attn"), check_vma=False
    )
```

time: 261 us -> 45.6 us (0.17)
  blocking collectives: 105 us -> 0 us
  waiting for transfers between devices: 103 us -> 0 us
  Pallas kernels: 0 us -> 43.6 us
  between operations: 14.9 us -> 0.66 us
  local copies, waits for them, and re-layouts: 14.4 us -> 1.26 us
  starting transfers between devices: 10.7 us -> 0 us
  matrix products: 10 us -> 0 us
    unnamed x2 -> x0, waiting for transfers between devices: 91.1 us -> none
    pallas_call x0 -> x1, Pallas kernels: none -> 43.6 us  [shards(): pl.pallas_call(kernel, out_shape=jax.ShapeDtypeStruct((4, COLS), BF16), i...]
    all_gather x2 -> x0, blocking collectives: 42.8 us -> none  [the longest x1 26.1 us: shards(): gathered = lax.all_gather(heads, ('attn', 'tp'), axis=0, tiled=True)]
    psum x2 -> x0, blocking collectives: 36.3 us -> none  [the longest x1 30.8 us: shards(): squares, logits = lax.psum((squares, partial_logits), 'attn')]
    unnamed x1 -> x0, blocking collectives: 25.8 us -> none
    all_to_all x2 -> x0, waiting for transfers between devices: 12.2 us -> none  [the longest x1 6.54 us: shards(): lax.all_to_all(outputs, 'expert', split_axis=0, concat_axis=0, tiled=True)]
    all_to_all x2 -> x0, starting transfers between devices: 10.7 us -> none  [the longest x1 6.74 us: shards(): lax.all_to_all(outputs, 'expert', split_axis=0, concat_axis=0, tiled=True)]
    dot_general x9 -> x0, matrix products: 10 us -> none  [the longest x1 3.81 us: shards(): jnp.einsum('esd,edcf->escf', inputs, up_weight, preferred_element_type=jn...]
  transfers between devices with their start and end apart: 3 -> 0, of which waited for: 3 -> 0; matrix products, arithmetic and copies ran while one was open for 1% -> 0% of each run, Pallas kernels for 0% -> 0%
where the time goes in v1:
time: 45.6 us; the launch traced here: 45.5 us
  Pallas kernels  43.6 us (96%)
  local copies, waits for them, and re-layouts  1.26 us (3%)
  between operations  0.66 us (1%)
    pallas_call x1, Pallas kernels, shards(): pl.pallas_call(kernel, out_shape=jax.ShapeDtypeStruct((4, COLS), BF16), i...  43.6 us
    unnamed x1, local copies, waits for them, and re-layouts  1.26 us

profile of v1, /device:TPU:1, one launch (start us, length us, event | category | flops | bytes accessed | tf_op | source)
XLA Modules:
  0.0 45.5 jit_solution(7953500935119887607)
XLA Ops:
  0.7 43.6 %shard_map.109 = bf16[4,384]{1,0:T(4,128)(2,1)} custom-call(bf16[4,384]{1,0:T(4,128)(2,1)} %tok_hbm.1, bf16[6,128]{1,0:T(8,128)(2,1)} %bitcast.12, bf16[4096,128]{1,0:T(8,128)(2,1)} %bitcast.9, bf16[4096,128]{1,0:T(8,128)(2,1)} %bitcast.10, s32[1]{0:T(128)S(6)} %copy.13.len_ref, bf16[768,384]{1,0:T(8,128)(2,1)} %wo_hbm.1, bf16[384]{0:T(512)(128)(2,1)} %gain_hbm.1, ...), custom_call_target="tpu_custom_call" | custom-call | tf_op jit(solution)/shard_map/pallas_call | solution.py:329
  44.2 1.3 %copy.14 = bf16[4,384]{1,0:T(4,128)(2,1)} copy(bf16[4,384]{1,0:T(4,128)(2,1)} %shard_map.109) | data formatting | bytes 6144

commit v2 on v1

--- a/solution.py
+++ b/solution.py
@@ -29,8 +29,8 @@
     tok_hbm, q_hbm, k_hbm, v_hbm, len_ref, wo_hbm, gain_hbm, router_hbm, routes_hbm, up_hbm, down_hbm,
     out_ref,
     tok, q, k, v, wo, gain, router, routes, up, up2, down,
-    heads, gath, zsum, resid, feats, stat, stats, stat_tot, hid, part, part_sib, reduced, back, ret_s, ret,
-    in_sem, p1_s, p1_r, p2_s, p2_r, p3_s, p3_r, fw_s, fw_r, st_s, st_r, sib_s, sib_r, p4x_s, p4x_r, p4_s, p4_r, p5_s, p5_r,
+    heads, gath, zsum, resid, feats, stat, stats, logit_half, reduced, back, ret_s, ret,
+    in_sem, p1_s, p1_r, p2_s, p2_r, p3_s, p3_r, st_s, st_r, sib_s, sib_r, w_s, w_r, dn_s, dn_r, p4_s, p4_r, p5_s, p5_r,
 ):
     a, e, t = lax.axis_index("attn"), lax.axis_index("expert"), lax.axis_index("tp")
     ay, ax = lax.div(a, 4), lax.rem(a, 4)
@@ -43,7 +43,7 @@
     pairs = (
         ("q", q_hbm, q), ("k", k_hbm, k), ("v", v_hbm, v), ("wo", wo_hbm, wo), ("tok", tok_hbm, tok),
         ("gain", gain_hbm, gain), ("router", router_hbm, router), ("routes", routes_hbm, routes),
-        ("up", up_hbm, up), ("down", down_hbm, down),
+        ("up", up_hbm, up), ("down", down_hbm, down.at[0]),
     )
     for n, (name, src, dst) in enumerate(pairs):
         loads[name] = pltpu.make_async_copy(src, dst, in_sem.at[n])
@@ -109,7 +109,11 @@
 
     def relayout(i, c):
         s = pl.ds(pl.multiple_of(i * COLS, COLS), COLS)
-        up2[:, s, :] = jnp.swapaxes(up[s].astype(F32), 0, 1).astype(BF16)
+        up2[0:2, s, :] = jnp.swapaxes(up[s].astype(F32), 0, 1).astype(BF16)
+        pltpu.make_async_remote_copy(
+            src_ref=up2.at[pl.ds(0, 2), s], dst_ref=up2.at[pl.ds(2, 2), s], send_sem=w_s, recv_sem=w_r.at[i],
+            device_id=sib, device_id_type=MESH,
+        ).start()
         return c
 
     lax.fori_loop(0, D // COLS, relayout, 0)
@@ -135,29 +139,25 @@
             src_ref=zsum.at[e], dst_ref=zsum.at[e], send_sem=p2_s, recv_sem=p2_r,
             device_id=(a, lax.rem(e + dz, NE), t), device_id_type=MESH,
         ).start()
+    down_copy = pltpu.make_async_remote_copy(
+        src_ref=down.at[0], dst_ref=down.at[1], send_sem=dn_s, recv_sem=dn_r, device_id=sib, device_id_type=MESH
+    )
+    down_copy.start()
     gains = gain[...].reshape(1, COLS).astype(F32)
     drain(zsum.at[pl.ds(0, 7)], p2_r)
     rounded = sum(zsum[i].astype(F32) for i in range(NE)).astype(BF16)
     wide = rounded.astype(F32)
     gained = wide * gains
-    feats[a, t] = gained.astype(BF16)
+    feats[a] = gained.astype(BF16)
 
     def feature_copy(o):
         return pltpu.make_async_remote_copy(
-            src_ref=feats.at[a, t], dst_ref=feats.at[a, t], send_sem=p3_s, recv_sem=p3_r.at[a],
+            src_ref=feats.at[a], dst_ref=feats.at[a], send_sem=p3_s, recv_sem=p3_r.at[a],
             device_id=(near(o), e, t), device_id_type=MESH,
         )
 
-    def forward_copy(o):
-        b = near(o)
-        return pltpu.make_async_remote_copy(
-            src_ref=feats.at[b, t], dst_ref=feats.at[b, t], send_sem=fw_s, recv_sem=fw_r.at[b],
-            device_id=sib, device_id_type=MESH,
-        )
-
     for o in NEAR[:0:-1]:
         feature_copy(o).start()
-    forward_copy((0, 0)).start()
     resid[t] = rounded
     resid_copy = pltpu.make_async_remote_copy(
         src_ref=resid.at[t], dst_ref=resid.at[t], send_sem=sib_s.at[0], recv_sem=sib_r.at[0],
@@ -179,75 +179,48 @@
         ).start()
     stats[a] = stat[...]
 
-    gate_acc = jnp.zeros((2 * HALF, HID), F32)
-    up_acc = jnp.zeros((2 * HALF, HID), F32)
-
-    def chunk(o, gate_acc, up_acc):
+    accs = [jnp.zeros((HALF, HID), F32)] * 4
+    for j, o in enumerate(NEAR):
         b = near(o)
-        drain(feats.at[b, 1 - t], fw_r.at[b])
-        x = jnp.concatenate([feats[b, 0], feats[b, 1]], axis=0)
+        if j > 0:
+            drain(feats.at[b], p3_r.at[b])
         s = pl.ds(pl.multiple_of(b * COLS, COLS), COLS)
-        gate_acc = gate_acc + jnp.dot(x, up2[0, s, :], preferred_element_type=F32)
-        up_acc = up_acc + jnp.dot(x, up2[1, s, :], preferred_element_type=F32)
-        return gate_acc, up_acc
-
-    LAG = 2
-    for j, o in enumerate(NEAR):
-        if j > 0:
-            drain(feats.at[near(o), t], p3_r.at[near(o)])
-            forward_copy(o).start()
-        if j >= LAG:
-            gate_acc, up_acc = chunk(NEAR[j - LAG], gate_acc, up_acc)
+        drain(up2.at[pl.ds(2, 2), s], w_r.at[b])
+        x = feats[b]
+        accs = [acc + jnp.dot(x, up2[i, s, :], preferred_element_type=F32) for i, acc in enumerate(accs)]
     drain(stats.at[pl.ds(0, 15)], st_r)
-    stat_tot[t] = sum(stats[i] for i in range(NA))
-    total_copy = pltpu.make_async_remote_copy(
-        src_ref=stat_tot.at[t], dst_ref=stat_tot.at[t], send_sem=sib_s.at[1], recv_sem=sib_r.at[1],
+    total_stat = sum(stats[i] for i in range(NA))
+    tots = jnp.concatenate([total_stat, pltpu.roll(total_stat, 64, 1)], axis=0)
+    scale = lax.rsqrt(tots[:, 8:9] / D + 1e-05)
+    accs = [acc * scale for acc in accs]
+    hidden = [(accs[i] * jax.nn.sigmoid(accs[i]) * accs[i + 1]).astype(BF16) for i in (0, 2)]
+    logit_half[t] = tots * scale
+    logit_copy = pltpu.make_async_remote_copy(
+        src_ref=logit_half.at[t], dst_ref=logit_half.at[t], send_sem=sib_s.at[1], recv_sem=sib_r.at[1],
         device_id=sib, device_id_type=MESH,
     )
-    total_copy.start()
-    for o in NEAR[NA - LAG :]:
-        gate_acc, up_acc = chunk(o, gate_acc, up_acc)
-    drain(stat_tot.at[1 - t], sib_r.at[1])
-    tots = jnp.concatenate(
-        [stat_tot[0], pltpu.roll(stat_tot[0], 64, 1), stat_tot[1], pltpu.roll(stat_tot[1], 64, 1)], axis=0
-    )
-    scale = lax.rsqrt(tots[:, 8:9] / D + 1e-05)
-    gate_acc, up_acc = gate_acc * scale, up_acc * scale
-    hidden = (gate_acc * jax.nn.sigmoid(gate_acc) * up_acc).astype(BF16)
-    hid[...] = hidden
-
-    def pair_copy(c):
-        s = pl.ds(4 * c, 4)
-        return pltpu.make_async_remote_copy(
-            src_ref=part.at[1 - t, s], dst_ref=part_sib.at[s], send_sem=p4x_s, recv_sem=p4x_r.at[c],
-            device_id=sib, device_id_type=MESH,
-        )
-
-    order = [lax.rem(ay + g, 4) for g in (2, 1, 3, 0)]
-    for c in order:
+
+    down_copy.wait_recv()
+    for g in (2, 1, 3, 0):
+        c = lax.rem(ay + g, 4)
         s = pl.ds(pl.multiple_of(c * (4 * COLS), 4 * COLS), 4 * COLS)
-        d = jnp.dot(hid[...], down[:, s], preferred_element_type=F32).astype(BF16)
+        d = sum(jnp.dot(hidden[i], down[i, :, s], preferred_element_type=F32) for i in range(2)).astype(BF16)
         for i in range(4):
-            part[0, 4 * c + i] = d[0:HALF, i * COLS : (i + 1) * COLS]
-            part[1, 4 * c + i] = d[HALF:, i * COLS : (i + 1) * COLS]
-        pair_copy(c).start()
-    for c in order:
-        drain(part_sib.at[pl.ds(4 * c, 4)], p4x_r.at[c])
-        for g in (2, 1, 3, 0):
-            b = 4 * c + lax.rem(ax + g, 4)
-            reduced[b] = (part[t, b].astype(F32) + part_sib[b].astype(F32)).astype(BF16)
-
-            @pl.when(b != a)
-            def _():
+            reduced[4 * c + i] = d[:, i * COLS : (i + 1) * COLS]
+        for i in (2, 1, 3, 0):
+            b = 4 * c + lax.rem(ax + i, 4)
+            if (g, i) != (0, 0):
                 pltpu.make_async_remote_copy(
                     src_ref=reduced.at[b], dst_ref=back.at[a], send_sem=p4_s, recv_sem=p4_r,
                     device_id=(b, e, t), device_id_type=MESH,
                 ).start()
-
     back[a] = reduced[a]
-
-    logits = tots * scale
-    own = sum(jnp.where(e == i, logits[4 * i : 4 * i + 4], 0.0) for i in range(NE))
+    logit_copy.start()
+
+    drain(logit_half.at[1 - t], sib_r.at[1])
+    own = sum(
+        jnp.where(e == 4 * h + i, logit_half[h, 4 * i : 4 * i + 4, :], 0.0) for h in range(2) for i in range(4)
+    )
     square = (4, 128)
     lanes = lax.broadcasted_iota(jnp.int32, square, 1)
     rows = lax.broadcasted_iota(jnp.int32, (4, 4), 0)
@@ -313,11 +286,11 @@
 
     drain(zsum.at[pl.ds(0, 7)], p2_s)
     drain(back.at[pl.ds(0, 15)], p3_s)
-    drain(back, fw_s)
     drain(stats.at[pl.ds(0, 15)], st_s)
     drain(resid.at[t], sib_s.at[0])
-    drain(stat_tot.at[t], sib_s.at[1])
-    drain(part_sib, p4x_s)
+    drain(logit_half.at[t], sib_s.at[1])
+    drain(up2.at[pl.ds(0, 2)], w_s)
+    down_copy.wait_send()
     drain(back.at[pl.ds(0, 15)], p4_s)
 
 
@@ -341,26 +314,23 @@
             pltpu.VMEM((NE, COLS), F32),
             pltpu.VMEM((2, 4), jnp.int32),
             pltpu.VMEM((D, 2, HID), BF16),
-            pltpu.VMEM((2, D, HID), BF16),
-            pltpu.VMEM((HID, D), BF16),
+            pltpu.VMEM((4, D, HID), BF16),
+            pltpu.VMEM((2, HID, D), BF16),
             pltpu.VMEM((8, HD), F32),
             pltpu.VMEM((HALF, 8, HD), F32),
             pltpu.VMEM((NE, HALF, COLS), BF16),
             pltpu.VMEM((NT, HALF, COLS), BF16),
-            pltpu.VMEM((NA, NT, HALF, COLS), BF16),
+            pltpu.VMEM((NA, HALF, COLS), BF16),
             pltpu.VMEM((8, 128), F32),
             pltpu.VMEM((NA, 8, 128), F32),
-            pltpu.VMEM((NT, 8, 128), F32),
-            pltpu.VMEM((2 * HALF, HID), BF16),
-            pltpu.VMEM((NT, NA, HALF, COLS), BF16),
-            pltpu.VMEM((NA, HALF, COLS), BF16),
+            pltpu.VMEM((NT, HALF, 128), F32),
             pltpu.VMEM((NA, HALF, COLS), BF16),
             pltpu.VMEM((NA, HALF, COLS), BF16),
             pltpu.VMEM((4, 4, COLS), F32),
             pltpu.VMEM((NE, 4, COLS), F32),
             dma((10,)),
-            dma, dma, dma, dma, dma, dma((NA,)), dma, dma((NA,)), dma, dma,
-            dma((2,)), dma((2,)), dma, dma((4,)), dma, dma, dma, dma,
+            dma, dma, dma, dma, dma, dma((NA,)), dma, dma, dma((2,)), dma((2,)),
+            dma, dma((NA,)), dma, dma, dma, dma, dma, dma,
         ],
         compiler_params=pltpu.CompilerParams(
             collective_id=0, has_side_effects=True, vmem_limit_bytes=63 << 20

time: 45.6 us -> 40.5 us (0.89)
  Pallas kernels: 43.6 us -> 38.5 us
    pallas_call x1, Pallas kernels: 43.6 us -> 38.5 us  [shards(): pl.pallas_call(kernel, out_shape=jax.ShapeDtypeStruct((4, COLS), BF16), i...]
where the time goes in v2:
time: 40.5 us; the launch traced here: 40.4 us
  Pallas kernels  38.5 us (95%)
  local copies, waits for them, and re-layouts  1.26 us (3%)
  between operations  0.66 us (2%)
    pallas_call x1, Pallas kernels, shards(): pl.pallas_call(kernel, out_shape=jax.ShapeDtypeStruct((4, COLS), BF16), i...  38.5 us
    unnamed x1, local copies, waits for them, and re-layouts  1.26 us

profile of v2, /device:TPU:1, one launch (start us, length us, event | category | flops | bytes accessed | tf_op | source)
XLA Modules:
  0.0 40.4 jit_solution(547623696792654109)
XLA Ops:
  0.7 38.5 %shard_map.109 = bf16[4,384]{1,0:T(4,128)(2,1)} custom-call(bf16[4,384]{1,0:T(4,128)(2,1)} %tok_hbm.1, bf16[6,128]{1,0:T(8,128)(2,1)} %bitcast.12, bf16[4096,128]{1,0:T(8,128)(2,1)} %bitcast.9, bf16[4096,128]{1,0:T(8,128)(2,1)} %bitcast.10, s32[1]{0:T(128)S(6)} %copy.13.len_ref, bf16[768,384]{1,0:T(8,128)(2,1)} %wo_hbm.1, bf16[384]{0:T(512)(128)(2,1)} %gain_hbm.1, ...), custom_call_target="tpu_custom_call" | custom-call | tf_op jit(solution)/shard_map/pallas_call | solution.py:302
  39.1 1.3 %copy.14 = bf16[4,384]{1,0:T(4,128)(2,1)} copy(bf16[4,384]{1,0:T(4,128)(2,1)} %shard_map.109) | data formatting | bytes 6144
